TPU v7x, 32 devices: a whole 2x2x4 slice. The times are simulated.
32 devices in a mesh: groups: 2 (over y), tensor: 2 (over core), expert: 8 (over z, x).
Axes of the slice: x: 2, y: 2, z: 4, core: 2. Of those that a mesh axis runs over, the one named last changes fastest.
Arguments:
- d_output: bfloat16 [4096, 4096], P(('groups', 'tensor', 'expert')), parts along dimension 0, may hold values from -6 to 6
- w_gate: bfloat16 [8, 4096, 704], P('expert', 'tensor'), may hold values from -0.875 to 0.875
- w_up: bfloat16 [8, 4096, 704], P('expert', 'tensor'), may hold values from -0.875 to 0.875
- w_down: bfloat16 [8, 704, 4096], P('expert', None, 'tensor'), may hold values from -0.0234375 to 0.0234375
- gate_pre: bfloat16 [8, 128, 704], P('expert', 'groups'), parts along dimension 1, may hold values from -6 to 6
- up_pre: bfloat16 [8, 128, 704], P('expert', 'groups'), parts along dimension 1, may hold values from -6 to 6
- gate_scores: float32 [8, 128], P('expert', 'groups'), parts along dimension 1, may hold values from 0.05 to 1
- slot_tokens: int32 [8, 8, 2, 8], P(None, 'expert', None, 'groups'), parts along dimension 3, may hold values from 0 to 127, as said below
- slot_counts: int32 [8, 8, 4], P(None, 'expert', 'groups'), parts along dimension 2, may hold values from 0 to 4, as said below
Outputs:
- d_tokens: bfloat16 [4096, 4096], P(('groups', 'tensor', 'expert')), parts along dimension 0
- d_scores: float32 [8, 128], P('expert', 'groups'), parts along dimension 1
There are 2 independent parts, one for each index of `groups`. A program takes and returns all parts, laid end to end along the dimension named above; an argument that names none is the same for every part. Nothing has to cross between parts.
Inputs may be any that keep to these rules, and one draw needn't show every extreme that they name: `slot_tokens`: the 4 entries of a block are distinct rows of the source device's 128 tokens; entries past the block's count are padding. `slot_counts`: in every draw some expert has all of its blocks full.
All inputs are finite; a program needn't handle non-finite values.
Results may differ from a plain program's by a relative error of at most 0.0051.
Values may be sent and summed in bfloat16 or wider, within the bound.
A program may use at most 64 MiB of HBM per device.

v0:
```python
import jax
import jax.numpy as jnp
from jax import lax
from jax.sharding import PartitionSpec as P


def expert_math(slot_rows, w_gate, w_up, w_down, gate_pre, up_pre, gate_scores):
    partial_value = lax.dot_general(
        slot_rows, w_down[0], (((1,), (1,)), ((), ())), preferred_element_type=jnp.float32
    )
    hidden_grad = lax.psum(partial_value, "tensor")
    gate_val = gate_pre[0].astype(jnp.float32)
    up_val = up_pre[0].astype(jnp.float32)
    sigmoid_g = jax.nn.sigmoid(gate_val)
    silu_g = gate_val * sigmoid_g
    scores = jnp.sum(silu_g * up_val * hidden_grad, axis=1)[None]
    d_hidden = gate_scores[0][:, None] * hidden_grad
    d_gate = (d_hidden * up_val * sigmoid_g * (1.0 + gate_val * (1.0 - sigmoid_g))).astype(
        jnp.bfloat16
    )
    d_up = (d_hidden * silu_g).astype(jnp.bfloat16)
    slot_grad = lax.dot_general(
        d_gate, w_gate[0], (((1,), (1,)), ((), ())), preferred_element_type=jnp.float32
    )
    slot_grad = slot_grad + lax.dot_general(
        d_up, w_up[0], (((1,), (1,)), ((), ())), preferred_element_type=jnp.float32
    )
    return (slot_grad.astype(jnp.bfloat16), scores)


def per_device(
    d_output, w_gate, w_up, w_down, gate_pre, up_pre, gate_scores, slot_tokens, slot_counts
):
    tok_rows = d_output.shape[0]
    width = d_output.shape[1]
    experts = slot_tokens.shape[0]
    core_count = slot_tokens.shape[2]
    pair_rows = slot_tokens.shape[3]
    routes = slot_tokens[:, 0]
    valid = lax.iota(jnp.int32, pair_rows)[None, None, :] < slot_counts[:, 0][..., None]
    my_core = lax.axis_index("tensor")
    my_routes = lax.dynamic_index_in_dim(routes, my_core, 1, keepdims=False)
    keep_mask = lax.dynamic_index_in_dim(valid, my_core, 1, keepdims=False)
    picked = jnp.take(d_output, my_routes.reshape(-1), axis=0).reshape(experts, pair_rows, width)
    sent_rows = jnp.where(keep_mask[..., None], picked, jnp.zeros((), jnp.bfloat16))
    arrived = lax.all_to_all(sent_rows, "expert", split_axis=0, concat_axis=0, tiled=True)
    arrived = lax.all_to_all(arrived[:, None], "tensor", split_axis=3, concat_axis=1, tiled=True)
    half_width = arrived.shape[-1]
    slot_grad, scores = expert_math(
        arrived.reshape(-1, half_width), w_gate, w_up, w_down, gate_pre, up_pre, gate_scores
    )
    returned = lax.all_to_all(
        slot_grad.reshape(experts, core_count, pair_rows, half_width),
        "tensor",
        split_axis=1,
        concat_axis=3,
        tiled=True,
    )
    returned = lax.all_to_all(returned[:, 0], "expert", split_axis=0, concat_axis=0, tiled=True)
    one_hot = (my_routes.reshape(-1)[None, :] == lax.iota(jnp.int32, tok_rows)[:, None]).astype(
        jnp.bfloat16
    )
    summed = jnp.dot(one_hot, returned.reshape(-1, width), preferred_element_type=jnp.float32)
    d_tokens = summed.astype(jnp.bfloat16)
    return (d_tokens, scores)


def solution(mesh):
    placed = (
        P(("groups", "tensor", "expert"), None),
        P("expert", "tensor", None),
        P("expert", "tensor", None),
        P("expert", None, "tensor"),
        P("expert", "groups", None),
        P("expert", "groups", None),
        P("expert", "groups"),
        P(None, "expert", None, "groups"),
        P(None, "expert", "groups"),
    )
    return jax.shard_map(
        per_device,
        mesh=mesh,
        in_specs=placed,
        out_specs=(P(("groups", "tensor", "expert"), None), P("expert", "groups")),
        check_vma=False,
    )
```

profile of v0, /device:TPU:0, one launch (start us, length us, event | category | flops | bytes accessed | tf_op | source)
XLA Modules:
  0.0 108.3 jit_solution(1814871452394974574)
XLA Ops:
  7.2 0.8 constant_dynamic-slice_fusion
  8.1 0.1 copy.44
  8.2 0.7 compare_and_fusion
  8.9 0.1 copy.45
  9.0 0.1 copy.43
  9.0 0.1 reshape.72
  9.1 2.3 %gather_fusion = bf16[32,4096]{1,0:T(8,128)(2,1)S(1)} fusion(bf16[128,4096]{1,0:T(8,128)(2,1)} %param.9, s32[1024]{0:T(1024)S(1)} %pad_clamp_fusion), kind=kCustom, calls=%fused_computation | custom fusion | bytes 524416 | tf_op jit(solution)/shard_map/jit(_take)/gather | solution.py:44
  11.5 0.1 gather.7
  11.6 0.2 select_select_fusion
  11.8 16.0 %all_to_all.40 = bf16[8,4,4096]{2,1,0:T(4,128)(2,1)S(1)} all-to-all(bf16[8,4,4096]{2,1,0:T(4,128)(2,1)S(1)} %select_select_fusion), channel_id=1, replica_groups=mesh['groups'=2,'tensor'=2,'expert'=8] {'expert'}, dimensions={0} | all-to-all | bytes 524288 | tf_op jit(solution)/shard_map/all_to_all | solution.py:46
  27.8 4.6 %copy.47 = bf16[8,1,4,4096]{0,2,1,3:T(4,128)(2,1)} copy(bf16[8,1,4,4096]{3,2,0,1:T(4,128)(2,1)S(1)} %bitcast.67) | data formatting | bytes 524288 | tf_op jit(solution)/shard_map/broadcast_in_dim | solution.py:47
  32.4 6.1 %reshape.87 = bf16[2,2,32768]{2,1,0:T(2,128)(2,1)S(1)} reshape(bf16[4096,1,4,8]{3,2,1,0:T(4,128)(2,1)} %bitcast.65) | data formatting | bytes 524288
  38.5 3.9 %all_to_all.41 = bf16[2,2,32768]{2,1,0:T(2,128)(2,1)S(1)} all-to-all(bf16[2,2,32768]{2,1,0:T(2,128)(2,1)S(1)} %reshape.87), channel_id=1, replica_groups=mesh['groups'=2,'tensor'=2,'expert'=8] {'tensor'}, dimensions={0} | all-to-all | bytes 524288 | tf_op jit(solution)/shard_map/all_to_all | solution.py:47
  42.5 6.1 %reshape.88 = bf16[4096,1,4,8]{3,2,1,0:T(4,128)(2,1)} reshape(bf16[2,2,32768]{2,1,0:T(2,128)(2,1)S(1)} %all_to_all.41) | data formatting | bytes 524288
  48.6 6.0 %copy.48 = bf16[8,1,4,2,2048]{4,2,3,0,1:T(4,128)(2,1)S(1)} copy(bf16[8,1,4,2,2048]{0,2,4,3,1:T(4,128)(2,1)} %bitcast.66) | data formatting | bytes 524288 | tf_op jit(solution)/shard_map/all_to_all | solution.py:47
  54.6 0.1 reshape.73
  54.7 3.5 %fusion.4 = f32[64,704]{1,0:T(8,128)} fusion(bf16[64,2048]{1,0:T(8,128)(2,1)S(1)} %reshape.73, bf16[1,704,2048]{2,1,0:T(8,128)(2,1)} %param.12), kind=kOutput, calls=%fused_computation.6 | convolution fusion | flops 184549376 | bytes 3325952 | tf_op jit(solution)/shard_map/dot_general | solution.py:8
  58.2 17.3 %all-reduce.2.cloned.1.call-done = f32[64,704]{1,0:T(8,128)} async-done(((f32[64,704]{1,0:T(8,128)}), f32[64,704]{1,0:T(8,128)}) %all-reduce.2.cloned.1.call-update) | async-done | bytes 180240 | tf_op jit(solution)/shard_map/psum | solution.py:11
  75.5 1.7 %fusion = f32[64,2048]{1,0:T(8,128)S(1)} fusion(bf16[1,2048,704]{1,2,0:T(8,128)(2,1)S(1)} %copy-done, f32[64,704]{1,0:T(8,128)} %all-reduce.2.cloned.1.call-done, f32[64]{0:T(128)S(1)} %bitcast.70, bf16[1,64,704]{2,1,0:T(8,128)(2,1)S(1)} %copy-done.3), kind=kOutput, calls=%fused_computation.2 | convolution fusion | flops 184909824 | bytes 3678464 | tf_op jit(solution)/shard_map/dot_general | solution.py:25
  77.2 0.1 copy-done.1
  77.4 0.7 fusion.9
  78.1 0.8 reshape.74
  78.9 1.0 copy.49
  79.9 3.9 %all_to_all.42 = bf16[8,2,4,2048]{3,2,0,1:T(4,128)(2,1)S(1)} all-to-all(bf16[8,2,4,2048]{3,2,0,1:T(4,128)(2,1)S(1)} %copy.49), channel_id=1, replica_groups=mesh['groups'=2,'tensor'=2,'expert'=8] {'tensor'}, dimensions={1} | all-to-all | bytes 524288 | tf_op jit(solution)/shard_map/all_to_all | solution.py:52
  83.9 0.3 copy.52
  84.2 0.9 reshape.86
  85.0 5.8 %all-to-all-start.3 = ((bf16[8,4,4096]{2,1,0:T(4,128)(2,1)}), bf16[8,4,4096]{2,1,0:T(4,128)(2,1)S(1)}, u32[]{:S(2)}, u32[]{:S(2)}) async-start(bf16[8,4,4096]{2,1,0:T(4,128)(2,1)} %reshape.86), calls=%async_computation.3 | async-start | bytes 524288 | tf_op jit(solution)/shard_map/all_to_all | solution.py:59
  90.8 0.1 eq.17
  90.9 1.6 %fusion.16 = f32[64]{0:T(128)} fusion(f32[64,704]{1,0:T(8,128)S(1)} %copy-done.2, bf16[1,64,704]{2,1,0:T(8,128)(2,1)} %param.14, bf16[1,64,704]{2,1,0:T(8,128)(2,1)S(1)} %copy-done.3), kind=kLoop, calls=%fused_computation.20 | loop fusion | flops 405440 | bytes 360704 | tf_op jit(solution)/shard_map/reduce_sum | solution.py:16
  92.5 7.6 %all-to-all-done.3 = bf16[8,4,4096]{2,1,0:T(4,128)(2,1)S(1)} async-done(((bf16[8,4,4096]{2,1,0:T(4,128)(2,1)}), bf16[8,4,4096]{2,1,0:T(4,128)(2,1)S(1)}, u32[]{:S(2)}, u32[]{:S(2)}) %all-to-all-start.3) | async-done | bytes 262176 | tf_op jit(solution)/shard_map/all_to_all | solution.py:59
  100.0 0.1 reshape.75
  100.1 1.4 %convolution_convert_fusion = bf16[128,4096]{1,0:T(8,128)(2,1)} fusion(bf16[32,4096]{1,0:T(8,128)(2,1)S(1)} %reshape.75, s32[32]{0:T(128)S(1)} %eq.17), kind=kOutput, calls=%fused_computation.1 | convolution fusion | flops 34082816 | bytes 1310848 | tf_op jit(solution)/shard_map/dot_general | solution.py:63
  (16 shorter events, 0.1 us)
Async XLA Ops:
  7.2 68.3 %copy-start = (bf16[1,2048,704]{1,2,0:T(8,128)(2,1)S(1)}, bf16[1,2048,704]{1,2,0:T(8,128)(2,1)}, u32[]{:S(2)}) copy-start(bf16[1,2048,704]{1,2,0:T(8,128)(2,1)} %param.11) | copy-start | bytes 8650756
  7.2 68.3 %all-reduce.2.cloned.1.call-start = ((), (), s32[]{:S(2)}) async-start(), calls=%async_computation.4 | async-start | bytes 393216 | tf_op jit(solution)/shard_map/psum | solution.py:11
  54.6 20.9 %copy-start.3 = (bf16[1,64,704]{2,1,0:T(8,128)(2,1)S(1)}, bf16[1,64,704]{2,1,0:T(8,128)(2,1)}, u32[]{:S(2)}) copy-start(bf16[1,64,704]{2,1,0:T(8,128)(2,1)} %param.13) | copy-start | bytes 270340
  54.6 20.9 %copy-start.5 = (f32[1,64]{1,0:T(1,128)S(1)}, f32[1,64]{1,0:T(1,128)}, u32[]{:S(2)}) copy-start(f32[1,64]{1,0:T(1,128)} %param.15) | copy-start | bytes 772
  75.5 1.9 %copy-start.1 = (bf16[1,2048,704]{1,2,0:T(8,128)(2,1)S(1)}, bf16[1,2048,704]{1,2,0:T(8,128)(2,1)}, u32[]{:S(2)}) copy-start(bf16[1,2048,704]{1,2,0:T(8,128)(2,1)} %param.10) | copy-start | bytes 8650756
  75.5 1.9 %copy-start.2 = (f32[64,704]{1,0:T(8,128)S(1)}, f32[64,704]{1,0:T(8,128)}, u32[]{:S(2)}) copy-start(f32[64,704]{1,0:T(8,128)} %all-reduce.2.cloned.1.call-done) | copy-start | bytes 540676
  75.5 1.9 %copy-start.4 = (bf16[1,64,704]{2,1,0:T(8,128)(2,1)S(1)}, bf16[1,64,704]{2,1,0:T(8,128)(2,1)}, u32[]{:S(2)}) copy-start(bf16[1,64,704]{2,1,0:T(8,128)(2,1)} %param.14) | copy-start | bytes 270340
  85.0 15.0 %all-to-all-start.3 = ((bf16[8,4,4096]{2,1,0:T(4,128)(2,1)}), bf16[8,4,4096]{2,1,0:T(4,128)(2,1)S(1)}, u32[]{:S(2)}, u32[]{:S(2)}) async-start(bf16[8,4,4096]{2,1,0:T(4,128)(2,1)} %reshape.86), calls=%async_computation.3 | async-start | bytes 524288 | tf_op jit(solution)/shard_map/all_to_all | solution.py:59
Sparse Core Ops, SparseCore 0:
  58.3 17.1 all-reduce.1
where the time goes:
time: 109 us; the launch traced here: 108 us
  local copies, waits for them, and re-layouts  29.8 us (27%)
  waiting for transfers between devices  24.8 us (23%)
  blocking collectives  23.9 us (22%)
  between operations  14.2 us (13%)
  matrix products  7.29 us (7%)
  starting transfers between devices  5.8 us (5%)
  other arithmetic  2.55 us (2%)
    psum x1, waiting for transfers between devices, expert_math(): hidden_grad = lax.psum(partial_value, 'tensor')  17.3 us
    all_to_all x1, blocking collectives, per_device(): lax.all_to_all(sent_rows, 'expert', split_axis=0, concat_axis=0, tiled=True)  16 us
    unnamed x14, local copies, waits for them, and re-layouts  12.4 us
    all_to_all x1, waiting for transfers between devices, per_device(): lax.all_to_all(returned[:, 0], 'expert', split_axis=0, concat_axis=0, til...  7.56 us
    all_to_all x1, local copies, waits for them, and re-layouts, per_device(): lax.all_to_all(arrived[:, None], 'tensor', split_axis=3, concat_axis=1, t...  6.01 us
    all_to_all x1, starting transfers between devices, per_device(): lax.all_to_all(returned[:, 0], 'expert', split_axis=0, concat_axis=0, til...  5.76 us
    broadcast_in_dim x1, local copies, waits for them, and re-layouts, per_device(): arrived[:, None]  4.59 us
    all_to_all x1, blocking collectives, per_device(): lax.all_to_all(arrived[:, None], 'tensor', split_axis=3, concat_axis=1, t...  3.94 us
  transfers between devices with their start and end apart: 2, of which 2 were waited for; matrix products, arithmetic and copies ran while one was open for 2% of the time, Pallas kernels for 0%

commit v1 on v0

v1 whole, which is shorter than its diff:
```python
import functools

import jax
import jax.numpy as jnp
from jax import lax
from jax.experimental import pallas as pl
from jax.experimental.pallas import tpu as pltpu
from jax.sharding import PartitionSpec as P

MESH = pl.DeviceIdType.MESH
TILE = 16
LANES = 128
F32 = jnp.float32
BF16 = jnp.bfloat16


def far_first(experts):
    offsets = []
    for step in range(experts):
        offset = experts // 2 + ((step + 1) // 2 if step % 2 else -(step // 2))
        offsets.append(offset % experts)
    return [k for k in offsets if k] + [0]


def put(wide, start, count, values):
    rows = wide.shape[0] // (values.shape[1] // LANES)
    for k in range(values.shape[1] // LANES):
        wide[pl.ds(k * rows + start, count, stride=TILE), :] = values[:, k * LANES : (k + 1) * LANES]


def get(wide, start, count, width):
    rows = wide.shape[0] // (width // LANES)
    return jnp.concatenate(
        [wide[pl.ds(k * rows + start, count, stride=TILE), :] for k in range(width // LANES)], axis=1
    )


def narrow(wide, block):
    rows, width = block.shape
    for k in range(width // LANES):
        block[:, k * LANES : (k + 1) * LANES] = wide[k * rows : (k + 1) * rows, :].astype(BF16)


def widen(block, wide):
    rows, width = block.shape
    for k in range(width // LANES):
        wide[k * rows : (k + 1) * rows, :] = block[:, k * LANES : (k + 1) * LANES].astype(F32)


def kernel(
    experts, pair,
    tok_hbm, cnt_hbm, d_hbm, wd_hbm, wg_hbm, wu_hbm, gate_hbm, up_hbm, gs_hbm,
    out_hbm, sc_ref,
    tok, cnt, d_v, wd, wg, wu, gate_b, up_b, gs,
    out_v, pick_f, send1, recv1, rows, hid_send, hid_recv, gate_f, up_f,
    back_f, send2, recv2,
    in_sem, out_sem, s1, r1, sh, rh, s2, r2,
):
    my_t = lax.axis_index("tensor")
    my_e = lax.axis_index("expert")
    n = 2 * experts
    half = wd.shape[2]
    groups = TILE // pair
    piece = half // groups
    tokens = d_v.shape[0]
    order = far_first(experts)

    barrier = pltpu.get_barrier_semaphore()
    peers = []
    for k in order:
        e = lax.rem(my_e + k, experts)
        for dt in (1, 0):
            if k == 0 and dt == 0:
                continue
            peers.append((e, lax.rem(my_t + dt, 2)))
    for e, t in peers:
        pl.semaphore_signal(
            barrier, inc=1, device_id={"tensor": t, "expert": e}, device_id_type=MESH
        )

    loads = []
    for i, (src, dst) in enumerate((
        (tok_hbm, tok), (cnt_hbm, cnt), (d_hbm, d_v), (gate_hbm, gate_b), (up_hbm, up_b),
        (gs_hbm, gs), (wd_hbm, wd), (wg_hbm, wg), (wu_hbm, wu),
    )):
        copy = pltpu.make_async_copy(src, dst, in_sem.at[i])
        copy.start()
        loads.append(copy)

    loads[0].wait()
    loads[1].wait()
    first = my_t == 0
    mine = jnp.where(first, tok[:, 0, 0, :], tok[:, 0, 1, :])
    count = jnp.where(first, cnt[:, 0, 0:1], cnt[:, 0, 1:2])
    lanes = lax.broadcasted_iota(jnp.int32, (experts, tokens), 1)
    parts = []
    for r in range(pair):
        hit = jnp.logical_and(lanes == mine[:, r : r + 1], count > r)
        parts.append(jnp.where(hit, 1.0, 0.0).astype(F32))
    one_hot_f = jnp.concatenate(parts, axis=0)
    one_hot = one_hot_f.astype(BF16)
    one_hot_t = one_hot_f.T.astype(BF16)

    loads[2].wait()
    for t in range(2):
        for c in range(groups):
            cols = slice(t * half + c * piece, t * half + (c + 1) * piece)
            got = jnp.dot(one_hot, d_v[:, cols], preferred_element_type=F32)
            for r in range(pair):
                put(
                    pick_f, t * experts * TILE + c * pair + r, experts,
                    got[r * experts : (r + 1) * experts],
                )
    narrow(pick_f, send1)

    me_flat = my_e * 2 + my_t
    pl.semaphore_wait(barrier, n - 1)

    def first_copy(i, e, t, lands):
        return pltpu.make_async_remote_copy(
            src_ref=send1.at[pl.ds(pl.multiple_of((t * experts + e) * TILE, TILE), TILE)],
            dst_ref=recv1.at[pl.ds(pl.multiple_of(lands * TILE, TILE), TILE)],
            send_sem=s1.at[i], recv_sem=r1.at[lands],
            device_id={"tensor": t, "expert": e}, device_id_type=MESH,
        )

    for i, (e, t) in enumerate(peers):
        first_copy(i, e, t, me_flat).start()
    own = pltpu.make_async_copy(
        send1.at[pl.ds(pl.multiple_of((my_t * experts + my_e) * TILE, TILE), TILE)],
        recv1.at[pl.ds(pl.multiple_of(me_flat * TILE, TILE), TILE)],
        in_sem.at[9],
    )
    own.start()

    for copy in loads[3:6]:
        copy.wait()
    src_id = lax.broadcasted_iota(jnp.int32, (n, n * pair), 0)
    slot_id = lax.broadcasted_iota(jnp.int32, (n, n * pair), 1)
    perm = jnp.concatenate(
        [jnp.where(slot_id == src_id * pair + r, 1.0, 0.0).astype(F32) for r in range(pair)], axis=0
    )
    perm_b = perm.astype(BF16)
    gate_val = jnp.dot(perm_b, gate_b[0], preferred_element_type=F32)
    up_val = jnp.dot(perm_b, up_b[0], preferred_element_type=F32)
    scale = jnp.sum(perm * gs[...], axis=1, keepdims=True)
    sig = jax.nn.sigmoid(gate_val)
    silu = gate_val * sig
    score_w = silu * up_val
    gate_w = up_val * sig * (1.0 + gate_val * (1.0 - sig))
    gate_f[...] = gate_w
    up_f[...] = silu

    loads[6].wait()
    own.wait()
    for i, (e, t) in enumerate(peers):
        first_copy(i, e, t, e * 2 + t).wait_recv()
    widen(recv1, back_f)
    for c in range(groups):
        for r in range(pair):
            rows[r * n : (r + 1) * n, c * piece : (c + 1) * piece] = get(
                back_f, c * pair + r, n, piece
            ).astype(BF16)

    hid_send[...] = lax.dot_general(
        rows[...], wd[0], (((1,), (1,)), ((), ())), preferred_element_type=F32
    )
    swap = pltpu.make_async_remote_copy(
        src_ref=hid_send, dst_ref=hid_recv, send_sem=sh, recv_sem=rh,
        device_id={"tensor": 1 - my_t, "expert": my_e}, device_id_type=MESH,
    )
    swap.start()
    loads[7].wait()
    loads[8].wait()
    swap.wait_recv()
    hidden = hid_send[...] + hid_recv[...]
    scores = jnp.sum(score_w * hidden, axis=1, keepdims=True)
    sc_ref[...] = jnp.sum(perm * scores, axis=0, keepdims=True)
    d_hidden = scale * hidden
    d_gate = (d_hidden * gate_f[...]).astype(BF16)
    d_up = (d_hidden * up_f[...]).astype(BF16)
    for c in range(groups):
        cols = slice(c * piece, (c + 1) * piece)
        part = lax.dot_general(
            d_gate, wg[0, cols, :], (((1,), (1,)), ((), ())), preferred_element_type=F32
        ) + lax.dot_general(
            d_up, wu[0, cols, :], (((1,), (1,)), ((), ())), preferred_element_type=F32
        )
        for r in range(pair):
            put(back_f, c * pair + r, n, part[r * n : (r + 1) * n])
    narrow(back_f, send2)

    my_place = my_t * experts + my_e

    def second_copy(i, e, t, lands):
        return pltpu.make_async_remote_copy(
            src_ref=send2.at[pl.ds(pl.multiple_of((e * 2 + t) * TILE, TILE), TILE)],
            dst_ref=recv2.at[pl.ds(pl.multiple_of(lands * TILE, TILE), TILE)],
            send_sem=s2.at[i], recv_sem=r2.at[lands],
            device_id={"tensor": t, "expert": e}, device_id_type=MESH,
        )

    for i, (e, t) in enumerate(peers):
        second_copy(i, e, t, my_place).start()
    own2 = pltpu.make_async_copy(
        send2.at[pl.ds(pl.multiple_of(me_flat * TILE, TILE), TILE)],
        recv2.at[pl.ds(pl.multiple_of(my_place * TILE, TILE), TILE)],
        in_sem.at[10],
    )
    own2.start()
    own2.wait()
    for i, (e, t) in enumerate(peers):
        second_copy(i, e, t, t * experts + e).wait_recv()
    widen(recv2, pick_f)
    stores = []
    for t in range(2):
        for c in range(groups):
            got = jnp.concatenate(
                [
                    get(pick_f, t * experts * TILE + c * pair + r, experts, piece)
                    for r in range(pair)
                ],
                axis=0,
            ).astype(BF16)
            cols = slice(t * half + c * piece, t * half + (c + 1) * piece)
            out_v[:, cols] = jnp.dot(one_hot_t, got, preferred_element_type=F32).astype(BF16)
            store = pltpu.make_async_copy(
                out_v.at[:, cols], out_hbm.at[:, cols], out_sem.at[t * groups + c]
            )
            store.start()
            stores.append(store)
    for i, (e, t) in enumerate(peers):
        first_copy(i, e, t, me_flat).wait_send()
        second_copy(i, e, t, my_place).wait_send()
    swap.wait_send()
    for store in stores:
        store.wait()


def per_device(
    d_output, w_gate, w_up, w_down, gate_pre, up_pre, gate_scores, slot_tokens, slot_counts
):
    tok_rows, width = d_output.shape
    experts = slot_tokens.shape[0]
    pair = slot_tokens.shape[3]
    hidden = w_down.shape[1]
    half = w_down.shape[2]
    n = 2 * experts
    slots = n * pair
    groups = TILE // pair
    piece = half // groups
    anywhere = pl.BlockSpec(memory_space=pl.ANY)
    dma = pltpu.SemaphoreType.DMA
    return pl.pallas_call(
        functools.partial(kernel, experts, pair),
        out_shape=(
            jax.ShapeDtypeStruct((tok_rows, width), BF16),
            jax.ShapeDtypeStruct((1, slots), F32),
        ),
        in_specs=[anywhere] * 9,
        out_specs=(anywhere, pl.BlockSpec(memory_space=pltpu.VMEM)),
        scratch_shapes=[
            pltpu.VMEM(slot_tokens.shape, jnp.int32),
            pltpu.VMEM(slot_counts.shape, jnp.int32),
            pltpu.VMEM(d_output.shape, BF16),
            pltpu.VMEM(w_down.shape, BF16),
            pltpu.VMEM(w_gate.shape, BF16),
            pltpu.VMEM(w_up.shape, BF16),
            pltpu.VMEM(gate_pre.shape, BF16),
            pltpu.VMEM(up_pre.shape, BF16),
            pltpu.VMEM(gate_scores.shape, F32),
            pltpu.VMEM((tok_rows, width), BF16),
            pltpu.VMEM((n * TILE * piece // LANES, LANES), F32),
            pltpu.VMEM((n * TILE, piece), BF16),
            pltpu.VMEM((n * TILE, piece), BF16),
            pltpu.VMEM((slots, half), BF16),
            pltpu.VMEM((slots, hidden), F32),
            pltpu.VMEM((slots, hidden), F32),
            pltpu.VMEM((slots, hidden), F32),
            pltpu.VMEM((slots, hidden), F32),
            pltpu.VMEM((n * TILE * piece // LANES, LANES), F32),
            pltpu.VMEM((n * TILE, piece), BF16),
            pltpu.VMEM((n * TILE, piece), BF16),
            dma((11,)),
            dma((2 * groups,)),
            dma((n,)),
            dma((n,)),
            dma,
            dma,
            dma((n,)),
            dma((n,)),
        ],
        compiler_params=pltpu.CompilerParams(
            collective_id=0, has_side_effects=True, vmem_limit_bytes=56 * 1024 * 1024
        ),
    )(
        slot_tokens, slot_counts, d_output, w_down, w_gate, w_up, gate_pre, up_pre, gate_scores
    )


def solution(mesh):
    placed = (
        P(("groups", "tensor", "expert"), None),
        P("expert", "tensor", None),
        P("expert", "tensor", None),
        P("expert", None, "tensor"),
        P("expert", "groups", None),
        P("expert", "groups", None),
        P("expert", "groups"),
        P(None, "expert", None, "groups"),
        P(None, "expert", "groups"),
    )
    return jax.shard_map(
        per_device,
        mesh=mesh,
        in_specs=placed,
        out_specs=(P(("groups", "tensor", "expert"), None), P("expert", "groups")),
        check_vma=False,
    )
```

time: 109 us -> 42.7 us (0.39)
  Pallas kernels: 0 us -> 28.1 us
  waiting for transfers between devices: 24.8 us -> 0 us
  blocking collectives: 23.9 us -> 0 us
  local copies, waits for them, and re-layouts: 29.8 us -> 13.7 us
  between operations: 14.2 us -> 0.64 us
  matrix products: 7.29 us -> 0 us
  starting transfers between devices: 5.8 us -> 0 us
  other arithmetic: 2.55 us -> 0 us
    pallas_call x0 -> x1, Pallas kernels: none -> 28.1 us  [per_device(): pl.pallas_call(functools.partial(kernel, experts, pair), out_shape=(jax.S...]
    all_to_all x3 -> x0, blocking collectives: 23.9 us -> none  [the longest x1 16 us: per_device(): lax.all_to_all(sent_rows, 'expert', split_axis=0, concat_axis=0, tiled=True)]
    psum x1 -> x0, waiting for transfers between devices: 17.3 us -> none  [expert_math(): hidden_grad = lax.psum(partial_value, 'tensor')]
    all_to_all x1 -> x0, waiting for transfers between devices: 7.56 us -> none  [per_device(): lax.all_to_all(returned[:, 0], 'expert', split_axis=0, concat_axis=0, til...]
    dot_general x4 -> x0, matrix products: 7.29 us -> none  [the longest x1 3.46 us: expert_math(): lax.dot_general(slot_rows, w_down[0], (((1,), (1,)), ((), ())), preferred...]
    all_to_all x1 -> x0, local copies, waits for them, and re-layouts: 6.01 us -> none  [per_device(): lax.all_to_all(arrived[:, None], 'tensor', split_axis=3, concat_axis=1, t...]
    all_to_all x1 -> x0, starting transfers between devices: 5.76 us -> none  [per_device(): lax.all_to_all(returned[:, 0], 'expert', split_axis=0, concat_axis=0, til...]
    broadcast_in_dim x2 -> x0, local copies, waits for them, and re-layouts: 4.69 us -> none  [the longest x1 4.59 us: per_device(): arrived[:, None]]
  transfers between devices with their start and end apart: 2 -> 0, of which waited for: 2 -> 0; matrix products, arithmetic and copies ran while one was open for 2% -> 0% of each run, Pallas kernels for 0% -> 0%
where the time goes in v1:
time: 42.7 us; the launch traced here: 42.4 us
  Pallas kernels  28.1 us (66%)
  local copies, waits for them, and re-layouts  13.7 us (32%)
  between operations  0.64 us (1%)
    pallas_call x1, Pallas kernels, per_device(): pl.pallas_call(functools.partial(kernel, experts, pair), out_shape=(jax.S...  28.1 us
    unnamed x8, local copies, waits for them, and re-layouts  13.7 us

profile of v1, /device:TPU:0, one launch (start us, length us, event | category | flops | bytes accessed | tf_op | source)
XLA Modules:
  0.0 42.4 jit_solution(126070655280483836)
XLA Ops:
  0.6 1.3 %copy.12.cnt_hbm = s32[8,1,2]{2,1,0:T(1,128)} copy(s32[8,1,2]{0,2,1:T(2,128)} %param.17) | data formatting | bytes 128 | tf_op args[8]
  2.0 1.4 %copy.11.tok_hbm = s32[8,1,2,4]{3,2,1,0:T(2,128)} copy(s32[8,1,2,4]{0,3,2,1:T(4,128)} %param.16) | data formatting | bytes 512 | tf_op args[7]
  3.3 0.0 copy-start
  3.3 4.7 %copy.13.wg_hbm = bf16[1,2048,704]{2,1,0:T(8,128)(2,1)} copy(bf16[1,2048,704]{1,2,0:T(8,128)(2,1)} %param.10) | data formatting | bytes 5767168 | tf_op args[1]
  8.1 0.0 copy-done
  8.1 2.8 %copy.14.wu_hbm = bf16[1,2048,704]{2,1,0:T(8,128)(2,1)} copy(bf16[1,2048,704]{1,2,0:T(8,128)(2,1)S(1)} %copy-done) | data formatting | bytes 5767168 | tf_op args[2]
  10.9 28.1 %shard_map.104 = (bf16[128,4096]{1,0:T(8,128)(2,1)}, f32[1,64]{1,0:T(1,128)}) custom-call(s32[8,1,2,4]{3,2,1,0:T(2,128)} %copy.11.tok_hbm, s32[8,1,2]{2,1,0:T(1,128)} %copy.12.cnt_hbm, bf16[128,4096]{1,0:T(8,128)(2,1)} %d_hbm.1, bf16[1,704,2048]{2,1,0:T(8,128)(2,1)} %wd_hbm.1, bf16[1,2048,704]{2,1,0:T(8,128)(2,1)} %copy.13.wg_hbm, ...), custom_call_target="tpu_custom_call" | custom-call | tf_op jit(solution)/shard_map/pallas_call | solution.py:254
  39.0 2.3 %copy.17 = bf16[128,4096]{1,0:T(8,128)(2,1)} copy(bf16[128,4096]{1,0:T(8,128)(2,1)} %get-tuple-element.4) | data formatting | bytes 2097152
  41.3 1.2 %copy.18 = f32[1,64]{1,0:T(1,128)} copy(f32[1,64]{1,0:T(1,128)} %get-tuple-element.5) | data formatting | bytes 512
Async XLA Ops:
  3.3 4.7 %copy-start = (bf16[1,2048,704]{1,2,0:T(8,128)(2,1)S(1)}, bf16[1,2048,704]{1,2,0:T(8,128)(2,1)}, u32[]{:S(2)}) copy-start(bf16[1,2048,704]{1,2,0:T(8,128)(2,1)} %param.11) | copy-start | bytes 8650756

commit v2 on v1

--- a/solution.py
+++ b/solution.py
@@ -47,14 +47,55 @@
         wide[k * rows : (k + 1) * rows, :] = block[:, k * LANES : (k + 1) * LANES].astype(F32)
 
 
+def picks(my_t, tok, cnt, tokens):
+    first = my_t == 0
+    mine = jnp.where(first, tok[0, 0], tok[0, 1])
+    count = jnp.where(first, cnt[0, 0:1, :], cnt[0, 1:2, :])
+    pair, experts = mine.shape
+    down = lax.broadcasted_iota(jnp.int32, (tokens, experts), 0)
+    parts = []
+    for r in range(pair):
+        hit = jnp.logical_and(down == mine[r : r + 1, :], count > r)
+        parts.append(jnp.where(hit, 1.0, 0.0).astype(F32))
+    return jnp.concatenate(parts, axis=1)
+
+
+def spread_kernel(experts, pair, tok, cnt, back, scores, out_hbm, sc_ref, out_v, wide, out_sem):
+    my_t = lax.axis_index("tensor")
+    groups = TILE // pair
+    tokens, width = out_v.shape
+    piece = width // 2 // groups
+    one_hot_t = picks(my_t, tok, cnt, tokens).astype(BF16)
+    sc_ref[...] = scores[...]
+    widen(back, wide)
+    stores = []
+    for t in range(2):
+        for c in range(groups):
+            got = jnp.concatenate(
+                [
+                    get(wide, t * experts * TILE + c * pair + r, experts, piece)
+                    for r in range(pair)
+                ],
+                axis=0,
+            ).astype(BF16)
+            i = t * groups + c
+            cols = slice(i * piece, (i + 1) * piece)
+            out_v[:, cols] = jnp.dot(one_hot_t, got, preferred_element_type=F32).astype(BF16)
+            store = pltpu.make_async_copy(out_v.at[:, cols], out_hbm.at[:, cols], out_sem.at[i])
+            store.start()
+            stores.append(store)
+    for store in stores:
+        store.wait()
+
+
 def kernel(
     experts, pair,
     tok_hbm, cnt_hbm, d_hbm, wd_hbm, wg_hbm, wu_hbm, gate_hbm, up_hbm, gs_hbm,
-    out_hbm, sc_ref,
+    recv2, sc_ref,
     tok, cnt, d_v, wd, wg, wu, gate_b, up_b, gs,
-    out_v, pick_f, send1, recv1, rows, hid_send, hid_recv, gate_f, up_f,
-    back_f, send2, recv2,
-    in_sem, out_sem, s1, r1, sh, rh, s2, r2,
+    pick_f, send1, recv1, rows, hid_send, hid_recv, gate_f, up_f,
+    back_f, send2,
+    in_sem, s1, r1, sh, rh, s2, r2,
 ):
     my_t = lax.axis_index("tensor")
     my_e = lax.axis_index("expert")
@@ -90,16 +131,7 @@
     loads[0].wait()
     loads[1].wait()
     first = my_t == 0
-    mine = jnp.where(first, tok[:, 0, 0, :], tok[:, 0, 1, :])
-    count = jnp.where(first, cnt[:, 0, 0:1], cnt[:, 0, 1:2])
-    lanes = lax.broadcasted_iota(jnp.int32, (experts, tokens), 1)
-    parts = []
-    for r in range(pair):
-        hit = jnp.logical_and(lanes == mine[:, r : r + 1], count > r)
-        parts.append(jnp.where(hit, 1.0, 0.0).astype(F32))
-    one_hot_f = jnp.concatenate(parts, axis=0)
-    one_hot = one_hot_f.astype(BF16)
-    one_hot_t = one_hot_f.T.astype(BF16)
+    one_hot = picks(my_t, tok, cnt, tokens).T.astype(BF16)
 
     loads[2].wait()
     for t in range(2):
@@ -182,9 +214,9 @@
     for c in range(groups):
         cols = slice(c * piece, (c + 1) * piece)
         part = lax.dot_general(
-            d_gate, wg[0, cols, :], (((1,), (1,)), ((), ())), preferred_element_type=F32
+            d_gate, wg[0, :, cols], (((1,), (0,)), ((), ())), preferred_element_type=F32
         ) + lax.dot_general(
-            d_up, wu[0, cols, :], (((1,), (1,)), ((), ())), preferred_element_type=F32
+            d_up, wu[0, :, cols], (((1,), (0,)), ((), ())), preferred_element_type=F32
         )
         for r in range(pair):
             put(back_f, c * pair + r, n, part[r * n : (r + 1) * n])
@@ -211,31 +243,10 @@
     own2.wait()
     for i, (e, t) in enumerate(peers):
         second_copy(i, e, t, t * experts + e).wait_recv()
-    widen(recv2, pick_f)
-    stores = []
-    for t in range(2):
-        for c in range(groups):
-            got = jnp.concatenate(
-                [
-                    get(pick_f, t * experts * TILE + c * pair + r, experts, piece)
-                    for r in range(pair)
-                ],
-                axis=0,
-            ).astype(BF16)
-            cols = slice(t * half + c * piece, t * half + (c + 1) * piece)
-            out_v[:, cols] = jnp.dot(one_hot_t, got, preferred_element_type=F32).astype(BF16)
-            store = pltpu.make_async_copy(
-                out_v.at[:, cols], out_hbm.at[:, cols], out_sem.at[t * groups + c]
-            )
-            store.start()
-            stores.append(store)
     for i, (e, t) in enumerate(peers):
         first_copy(i, e, t, me_flat).wait_send()
         second_copy(i, e, t, my_place).wait_send()
     swap.wait_send()
-    for store in stores:
-        store.wait()
-
 
 def per_device(
     d_output, w_gate, w_up, w_down, gate_pre, up_pre, gate_scores, slot_tokens, slot_counts
@@ -249,40 +260,44 @@
     slots = n * pair
     groups = TILE // pair
     piece = half // groups
-    anywhere = pl.BlockSpec(memory_space=pl.ANY)
+    anywhere = pl.BlockSpec(memory_space=pltpu.HBM)
     dma = pltpu.SemaphoreType.DMA
-    return pl.pallas_call(
+    routes = slot_tokens.transpose(1, 2, 3, 0)
+    counts = slot_counts.transpose(1, 2, 0)
+    gate_t = w_gate.swapaxes(1, 2)
+    up_t = w_up.swapaxes(1, 2)
+    block = (n * TILE, piece)
+    wide = (n * TILE * piece // LANES, LANES)
+    here = pl.BlockSpec(memory_space=pltpu.VMEM)
+    back, scores = pl.pallas_call(
         functools.partial(kernel, experts, pair),
         out_shape=(
-            jax.ShapeDtypeStruct((tok_rows, width), BF16),
+            jax.ShapeDtypeStruct(block, BF16),
             jax.ShapeDtypeStruct((1, slots), F32),
         ),
         in_specs=[anywhere] * 9,
-        out_specs=(anywhere, pl.BlockSpec(memory_space=pltpu.VMEM)),
+        out_specs=(here, here),
         scratch_shapes=[
-            pltpu.VMEM(slot_tokens.shape, jnp.int32),
-            pltpu.VMEM(slot_counts.shape, jnp.int32),
+            pltpu.VMEM(routes.shape, jnp.int32),
+            pltpu.VMEM(counts.shape, jnp.int32),
             pltpu.VMEM(d_output.shape, BF16),
             pltpu.VMEM(w_down.shape, BF16),
-            pltpu.VMEM(w_gate.shape, BF16),
-            pltpu.VMEM(w_up.shape, BF16),
+            pltpu.VMEM(gate_t.shape, BF16),
+            pltpu.VMEM(up_t.shape, BF16),
             pltpu.VMEM(gate_pre.shape, BF16),
             pltpu.VMEM(up_pre.shape, BF16),
             pltpu.VMEM(gate_scores.shape, F32),
-            pltpu.VMEM((tok_rows, width), BF16),
-            pltpu.VMEM((n * TILE * piece // LANES, LANES), F32),
-            pltpu.VMEM((n * TILE, piece), BF16),
-            pltpu.VMEM((n * TILE, piece), BF16),
+            pltpu.VMEM(wide, F32),
+            pltpu.VMEM(block, BF16),
+            pltpu.VMEM(block, BF16),
             pltpu.VMEM((slots, half), BF16),
             pltpu.VMEM((slots, hidden), F32),
             pltpu.VMEM((slots, hidden), F32),
             pltpu.VMEM((slots, hidden), F32),
             pltpu.VMEM((slots, hidden), F32),
-            pltpu.VMEM((n * TILE * piece // LANES, LANES), F32),
-            pltpu.VMEM((n * TILE, piece), BF16),
-            pltpu.VMEM((n * TILE, piece), BF16),
+            pltpu.VMEM(wide, F32),
+            pltpu.VMEM(block, BF16),
             dma((11,)),
-            dma((2 * groups,)),
             dma((n,)),
             dma((n,)),
             dma,
@@ -291,11 +306,26 @@
             dma((n,)),
         ],
         compiler_params=pltpu.CompilerParams(
-            collective_id=0, has_side_effects=True, vmem_limit_bytes=56 * 1024 * 1024
+            collective_id=0, has_side_effects=True, vmem_limit_bytes=63 * 1024 * 1024
         ),
     )(
-        slot_tokens, slot_counts, d_output, w_down, w_gate, w_up, gate_pre, up_pre, gate_scores
-    )
+        routes, counts, d_output, w_down, gate_t, up_t, gate_pre, up_pre, gate_scores
+    )
+    return pl.pallas_call(
+        functools.partial(spread_kernel, experts, pair),
+        out_shape=(
+            jax.ShapeDtypeStruct((tok_rows, width), BF16),
+            jax.ShapeDtypeStruct((1, slots), F32),
+        ),
+        in_specs=[here] * 4,
+        out_specs=(anywhere, here),
+        scratch_shapes=[
+            pltpu.VMEM((tok_rows, width), BF16),
+            pltpu.VMEM(wide, F32),
+            dma((2 * groups,)),
+        ],
+        compiler_params=pltpu.CompilerParams(vmem_limit_bytes=40 * 1024 * 1024),
+    )(routes, counts, back, scores)
 
 
 def solution(mesh):

time: 42.7 us -> 30.4 us (0.71)
  local copies, waits for them, and re-layouts: 13.7 us -> 1.55 us
    unnamed x8, local copies, waits for them, and re-layouts: 13.7 us -> 1.55 us
    pallas_call x1, Pallas kernels: 28.1 us -> 26.2 us  [per_device(): pl.pallas_call(functools.partial(kernel, experts, pair), out_shape=(jax.S...]
    pallas_call x0 -> x1, Pallas kernels: none -> 1.79 us  [per_device(): pl.pallas_call(functools.partial(spread_kernel, experts, pair), out_shape...]
where the time goes in v2:
time: 30.4 us; the launch traced here: 30.3 us
  Pallas kernels  28 us (92%)
  local copies, waits for them, and re-layouts  1.55 us (5%)
  between operations  0.68 us (2%)
    pallas_call x1, Pallas kernels, per_device(): pl.pallas_call(functools.partial(kernel, experts, pair), out_shape=(jax.S...  26.2 us
    pallas_call x1, Pallas kernels, per_device(): pl.pallas_call(functools.partial(spread_kernel, experts, pair), out_shape...  1.79 us
    unnamed x8, local copies, waits for them, and re-layouts  1.55 us

profile of v2, /device:TPU:0, one launch (start us, length us, event | category | flops | bytes accessed | tf_op | source)
XLA Modules:
  0.0 30.3 jit_solution(4485071725126013827)
XLA Ops:
  0.6 0.0 copy-start.1
  0.6 0.0 copy-start.2
  0.7 26.2 %shard_map.104 = (bf16[256,512]{1,0:T(8,128)(2,1)}, f32[1,64]{1,0:T(1,128)}) custom-call(s32[1,2,4,8]{3,2,1,0:T(4,128)} %bitcast.4, s32[1,2,8]{2,1,0:T(2,128)} %bitcast.6, bf16[128,4096]{1,0:T(8,128)(2,1)} %d_hbm.1, bf16[1,704,2048]{2,1,0:T(8,128)(2,1)} %wd_hbm.1, bf16[1,704,2048]{2,1,0:T(8,128)(2,1)} %bitcast.8, bf16[1,704,2048]{2,1,0:T(8,128)(2,1)} %bitcast.9, ...), custom_call_target="tpu_custom_call" | custom-call | tf_op jit(solution)/shard_map/pallas_call | solution.py:272
  26.9 0.0 copy-done.1
  26.9 0.0 copy-done.2
  26.9 0.0 copy-start
  26.9 0.9 %copy-done = bf16[256,512]{1,0:T(8,128)(2,1)S(1)} copy-done((bf16[256,512]{1,0:T(8,128)(2,1)S(1)}, bf16[256,512]{1,0:T(8,128)(2,1)}, u32[]{:S(2)}) %copy-start) | copy-done | bytes 262168
  27.9 0.0 copy-start.3
  27.9 0.6 %copy-done.3 = f32[1,64]{1,0:T(1,128)S(1)} copy-done((f32[1,64]{1,0:T(1,128)S(1)}, f32[1,64]{1,0:T(1,128)}, u32[]{:S(2)}) %copy-start.3) | copy-done | bytes 280
  28.5 1.8 %shard_map.105 = (bf16[128,4096]{1,0:T(8,128)(2,1)}, f32[1,64]{1,0:T(1,128)}) custom-call(s32[1,2,4,8]{3,2,1,0:T(4,128)S(1)} %bitcast.5, s32[1,2,8]{2,1,0:T(2,128)S(1)} %bitcast.7, bf16[256,512]{1,0:T(8,128)(2,1)S(1)} %copy-done, f32[1,64]{1,0:T(1,128)S(1)} %copy-done.3), custom_call_target="tpu_custom_call" | custom-call | tf_op jit(solution)/shard_map/pallas_call | solution.py:314
Async XLA Ops:
  0.6 26.3 %copy-start.1 = (s32[8,1,2,4]{0,3,2,1:T(4,128)S(1)}, s32[8,1,2,4]{0,3,2,1:T(4,128)}, u32[]{:S(2)}) copy-start(s32[8,1,2,4]{0,3,2,1:T(4,128)} %param.16) | copy-start | bytes 772
  0.6 26.3 %copy-start.2 = (s32[8,1,2]{0,2,1:T(2,128)S(1)}, s32[8,1,2]{0,2,1:T(2,128)}, u32[]{:S(2)}) copy-start(s32[8,1,2]{0,2,1:T(2,128)} %param.17) | copy-start | bytes 196
  26.9 1.0 %copy-start = (bf16[256,512]{1,0:T(8,128)(2,1)S(1)}, bf16[256,512]{1,0:T(8,128)(2,1)}, u32[]{:S(2)}) copy-start(bf16[256,512]{1,0:T(8,128)(2,1)} %get-tuple-element.4.back) | copy-start | bytes 786436
  27.9 0.6 %copy-start.3 = (f32[1,64]{1,0:T(1,128)S(1)}, f32[1,64]{1,0:T(1,128)}, u32[]{:S(2)}) copy-start(f32[1,64]{1,0:T(1,128)} %get-tuple-element.5.scores) | copy-start | bytes 772

commit v3 on v2

v3 whole, which is shorter than its diff:
```python
import functools

import jax
import jax.numpy as jnp
from jax import lax
from jax.experimental import pallas as pl
from jax.experimental.pallas import tpu as pltpu
from jax.sharding import PartitionSpec as P

MESH = pl.DeviceIdType.MESH
TILE = 16
LANES = 128
SPLITS = 2
F32 = jnp.float32
BF16 = jnp.bfloat16


def far_first(experts):
    offsets = []
    for step in range(experts):
        offset = experts // 2 + ((step + 1) // 2 if step % 2 else -(step // 2))
        offsets.append(offset % experts)
    return [k for k in offsets if k] + [0]


def put(wide, start, count, values):
    rows = wide.shape[0] // (values.shape[1] // LANES)
    for k in range(values.shape[1] // LANES):
        wide[pl.ds(k * rows + start, count, stride=TILE), :] = values[:, k * LANES : (k + 1) * LANES]


def get(wide, start, count, width):
    rows = wide.shape[0] // (width // LANES)
    return jnp.concatenate(
        [wide[pl.ds(k * rows + start, count, stride=TILE), :] for k in range(width // LANES)], axis=1
    )


def narrow(wide, block, base, count):
    rows, width = block.shape
    for k in range(width // LANES):
        block[base : base + count, k * LANES : (k + 1) * LANES] = wide[
            k * rows + base : k * rows + base + count, :
        ].astype(BF16)


def widen(block, wide, base, count):
    rows, width = block.shape
    for k in range(width // LANES):
        wide[k * rows + base : k * rows + base + count, :] = block[
            base : base + count, k * LANES : (k + 1) * LANES
        ].astype(F32)


def picks(my_t, tok, cnt, tokens):
    first = my_t == 0
    mine = jnp.where(first, tok[0, 0], tok[0, 1])
    count = jnp.where(first, cnt[0, 0:1, :], cnt[0, 1:2, :])
    pair, experts = mine.shape
    down = lax.broadcasted_iota(jnp.int32, (tokens, experts), 0)
    parts = []
    for r in range(pair):
        hit = jnp.logical_and(down == mine[r : r + 1, :], count > r)
        parts.append(jnp.where(hit, 1.0, 0.0).astype(F32))
    return jnp.concatenate(parts, axis=1)


def spread_kernel(experts, pair, tok, cnt, back, scores, out_hbm, sc_ref, out_v, wide, out_sem):
    my_t = lax.axis_index("tensor")
    tokens, width = out_v.shape
    part = pair // SPLITS
    groups = TILE // part
    piece = width // 2 // groups
    held = 2 * experts * TILE
    one_hot_t = picks(my_t, tok, cnt, tokens).astype(BF16)
    sc_ref[...] = scores[...]
    widen(back, wide, 0, SPLITS * held)
    stores = []
    for t in range(2):
        for c in range(groups):
            got = jnp.concatenate(
                [
                    get(
                        wide,
                        r // part * held + t * experts * TILE + c * part + r % part,
                        experts,
                        piece,
                    )
                    for r in range(pair)
                ],
                axis=0,
            ).astype(BF16)
            i = t * groups + c
            cols = slice(i * piece, (i + 1) * piece)
            out_v[:, cols] = jnp.dot(one_hot_t, got, preferred_element_type=F32).astype(BF16)
            store = pltpu.make_async_copy(out_v.at[:, cols], out_hbm.at[:, cols], out_sem.at[i])
            store.start()
            stores.append(store)
    for store in stores:
        store.wait()


def kernel(
    experts, pair,
    tok_hbm, cnt_hbm, d_hbm, wd_hbm, wg_hbm, wu_hbm, gate_hbm, up_hbm, gs_hbm,
    recv2, sc_ref,
    tok, cnt, d_v, wd, wg, wu, gate_b, up_b, gs,
    pick_f, send1, recv1, rows, hid_send, hid_recv, gate_f, up_f, score_f,
    back_f, send2,
    in_sem, s1, r1, sh, rh, s2, r2,
):
    my_t = lax.axis_index("tensor")
    my_e = lax.axis_index("expert")
    n = 2 * experts
    half = wd.shape[2]
    part = pair // SPLITS
    groups = TILE // part
    piece = half // groups
    held = n * TILE
    tokens = d_v.shape[0]
    order = far_first(experts)

    barrier = pltpu.get_barrier_semaphore()
    peers = []
    for k in order:
        e = lax.rem(my_e + k, experts)
        for dt in (1, 0):
            if k == 0 and dt == 0:
                continue
            peers.append((e, lax.rem(my_t + dt, 2)))
    for e, t in peers:
        pl.semaphore_signal(
            barrier, inc=1, device_id={"tensor": t, "expert": e}, device_id_type=MESH
        )

    def load(i, src, dst):
        copy = pltpu.make_async_copy(src, dst, in_sem.at[i])
        copy.start()
        return copy

    routes = [load(0, tok_hbm, tok), load(1, cnt_hbm, cnt)]
    halves = [
        load(2 + t, d_hbm.at[:, t * half : (t + 1) * half], d_v.at[:, t * half : (t + 1) * half])
        for t in range(2)
    ]
    for copy in routes:
        copy.wait()
    one_hot = picks(my_t, tok, cnt, tokens).T.astype(BF16)

    def pick(s):
        chosen = one_hot[s * part * experts : (s + 1) * part * experts]
        for t in range(2):
            if s == 0:
                halves[t].wait()
            for c in range(groups):
                cols = slice(t * half + c * piece, t * half + (c + 1) * piece)
                got = jnp.dot(chosen, d_v[:, cols], preferred_element_type=F32)
                for r in range(part):
                    put(
                        pick_f, s * held + t * experts * TILE + c * part + r, experts,
                        got[r * experts : (r + 1) * experts],
                    )
        narrow(pick_f, send1, s * held, held)

    me_flat = my_e * 2 + my_t
    my_place = my_t * experts + my_e

    def block(ref, s, place):
        return ref.at[pl.ds(pl.multiple_of(s * held + place * TILE, TILE), TILE)]

    def first_copy(s, i, e, t, lands):
        return pltpu.make_async_remote_copy(
            src_ref=block(send1, s, t * experts + e), dst_ref=block(recv1, s, lands),
            send_sem=s1.at[s, i], recv_sem=r1.at[s, lands],
            device_id={"tensor": t, "expert": e}, device_id_type=MESH,
        )

    def second_copy(s, i, e, t, lands):
        return pltpu.make_async_remote_copy(
            src_ref=block(send2, s, e * 2 + t), dst_ref=block(recv2, s, lands),
            send_sem=s2.at[s, i], recv_sem=r2.at[s, lands],
            device_id={"tensor": t, "expert": e}, device_id_type=MESH,
        )

    own1, own2, swaps = [], [], []
    weights = []
    for s in range(SPLITS):
        pick(s)
        if s == 0:
            pl.semaphore_wait(barrier, n - 1)
        for i, (e, t) in enumerate(peers):
            first_copy(s, i, e, t, me_flat).start()
        own1.append(load(9 + s, block(send1, s, my_place), block(recv1, s, me_flat)))
        if s == 0:
            small = [load(4, gate_hbm, gate_b), load(5, up_hbm, up_b), load(6, gs_hbm, gs)]
            weights = [load(7, wd_hbm, wd), load(8, wg_hbm, wg), load(9 + 2 * SPLITS, wu_hbm, wu)]

    for copy in small:
        copy.wait()
    src_id = lax.broadcasted_iota(jnp.int32, (n, n * pair), 0)
    slot_id = lax.broadcasted_iota(jnp.int32, (n, n * pair), 1)
    perm = jnp.concatenate(
        [jnp.where(slot_id == src_id * pair + r, 1.0, 0.0).astype(F32) for r in range(pair)], axis=0
    )
    perm_b = perm.astype(BF16)
    gate_val = jnp.dot(perm_b, gate_b[0], preferred_element_type=F32)
    up_val = jnp.dot(perm_b, up_b[0], preferred_element_type=F32)
    scale = jnp.sum(perm * gs[...], axis=1, keepdims=True)
    sig = jax.nn.sigmoid(gate_val)
    silu = gate_val * sig
    score_f[...] = silu * up_val
    gate_f[...] = scale * (up_val * sig * (1.0 + gate_val * (1.0 - sig)))
    up_f[...] = scale * silu

    weights[0].wait()
    count = part * n
    total = jnp.zeros((1, n * pair), F32)
    for s in range(SPLITS):
        own1[s].wait()
        for i, (e, t) in enumerate(peers):
            first_copy(s, i, e, t, e * 2 + t).wait_recv()
        mine = slice(s * count, (s + 1) * count)
        widen(recv1, back_f, s * held, held)
        for c in range(groups):
            for r in range(part):
                rows[s * count + r * n : s * count + (r + 1) * n, c * piece : (c + 1) * piece] = get(
                    back_f, s * held + c * part + r, n, piece
                ).astype(BF16)
        hid_send[mine] = lax.dot_general(
            rows[mine], wd[0], (((1,), (1,)), ((), ())), preferred_element_type=F32
        )
        swap = pltpu.make_async_remote_copy(
            src_ref=hid_send.at[mine], dst_ref=hid_recv.at[mine],
            send_sem=sh.at[s], recv_sem=rh.at[s],
            device_id={"tensor": 1 - my_t, "expert": my_e}, device_id_type=MESH,
        )
        swap.start()
        swaps.append(swap)
        if s == 0:
            weights[1].wait()
            weights[2].wait()
        swap.wait_recv()
        hidden = hid_send[mine] + hid_recv[mine]
        d_gate = (hidden * gate_f[mine]).astype(BF16)
        d_up = (hidden * up_f[mine]).astype(BF16)
        for c in range(groups):
            cols = slice(c * piece, (c + 1) * piece)
            summed = jnp.dot(
                d_gate, wg[0, :, cols], preferred_element_type=F32
            ) + jnp.dot(d_up, wu[0, :, cols], preferred_element_type=F32)
            for r in range(part):
                put(back_f, s * held + c * part + r, n, summed[r * n : (r + 1) * n])
        narrow(back_f, send2, s * held, held)
        for i, (e, t) in enumerate(peers):
            second_copy(s, i, e, t, my_place).start()
        own2.append(
            load(9 + SPLITS + s, block(send2, s, me_flat), block(recv2, s, my_place))
        )
        scores = jnp.sum(score_f[mine] * hidden, axis=1, keepdims=True)
        total = total + jnp.sum(perm[mine] * scores, axis=0, keepdims=True)
    sc_ref[...] = total
    for s in range(SPLITS):
        for i, (e, t) in enumerate(peers):
            first_copy(s, i, e, t, me_flat).wait_send()
        swaps[s].wait_send()
    for s in range(SPLITS):
        own2[s].wait()
        for i, (e, t) in enumerate(peers):
            second_copy(s, i, e, t, t * experts + e).wait_recv()
            second_copy(s, i, e, t, my_place).wait_send()


def per_device(
    d_output, w_gate, w_up, w_down, gate_pre, up_pre, gate_scores, slot_tokens, slot_counts
):
    tok_rows, width = d_output.shape
    experts = slot_tokens.shape[0]
    pair = slot_tokens.shape[3]
    hidden = w_down.shape[1]
    half = w_down.shape[2]
    n = 2 * experts
    slots = n * pair
    groups = TILE // (pair // SPLITS)
    piece = half // groups
    anywhere = pl.BlockSpec(memory_space=pltpu.HBM)
    dma = pltpu.SemaphoreType.DMA
    routes = slot_tokens.transpose(1, 2, 3, 0)
    counts = slot_counts.transpose(1, 2, 0)
    gate_t = w_gate.swapaxes(1, 2)
    up_t = w_up.swapaxes(1, 2)
    block = (SPLITS * n * TILE, piece)
    wide = (SPLITS * n * TILE * piece // LANES, LANES)
    here = pl.BlockSpec(memory_space=pltpu.VMEM)
    back, scores = pl.pallas_call(
        functools.partial(kernel, experts, pair),
        out_shape=(
            jax.ShapeDtypeStruct(block, BF16),
            jax.ShapeDtypeStruct((1, slots), F32),
        ),
        in_specs=[anywhere] * 9,
        out_specs=(here, here),
        scratch_shapes=[
            pltpu.VMEM(routes.shape, jnp.int32),
            pltpu.VMEM(counts.shape, jnp.int32),
            pltpu.VMEM(d_output.shape, BF16),
            pltpu.VMEM(w_down.shape, BF16),
            pltpu.VMEM(gate_t.shape, BF16),
            pltpu.VMEM(up_t.shape, BF16),
            pltpu.VMEM(gate_pre.shape, BF16),
            pltpu.VMEM(up_pre.shape, BF16),
            pltpu.VMEM(gate_scores.shape, F32),
            pltpu.VMEM(wide, F32),
            pltpu.VMEM(block, BF16),
            pltpu.VMEM(block, BF16),
            pltpu.VMEM((slots, half), BF16),
            pltpu.VMEM((slots, hidden), F32),
            pltpu.VMEM((slots, hidden), F32),
            pltpu.VMEM((slots, hidden), F32),
            pltpu.VMEM((slots, hidden), F32),
            pltpu.VMEM((slots, hidden), F32),
            pltpu.VMEM(wide, F32),
            pltpu.VMEM(block, BF16),
            dma((10 + 2 * SPLITS,)),
            dma((SPLITS, n)),
            dma((SPLITS, n)),
            dma((SPLITS,)),
            dma((SPLITS,)),
            dma((SPLITS, n)),
            dma((SPLITS, n)),
        ],
        compiler_params=pltpu.CompilerParams(
            collective_id=0, has_side_effects=True, vmem_limit_bytes=63 * 1024 * 1024
        ),
    )(
        routes, counts, d_output, w_down, gate_t, up_t, gate_pre, up_pre, gate_scores
    )
    return pl.pallas_call(
        functools.partial(spread_kernel, experts, pair),
        out_shape=(
            jax.ShapeDtypeStruct((tok_rows, width), BF16),
            jax.ShapeDtypeStruct((1, slots), F32),
        ),
        in_specs=[here] * 4,
        out_specs=(anywhere, here),
        scratch_shapes=[
            pltpu.VMEM((tok_rows, width), BF16),
            pltpu.VMEM(wide, F32),
            dma((2 * groups,)),
        ],
        compiler_params=pltpu.CompilerParams(vmem_limit_bytes=40 * 1024 * 1024),
    )(routes, counts, back, scores)


def solution(mesh):
    placed = (
        P(("groups", "tensor", "expert"), None),
        P("expert", "tensor", None),
        P("expert", "tensor", None),
        P("expert", None, "tensor"),
        P("expert", "groups", None),
        P("expert", "groups", None),
        P("expert", "groups"),
        P(None, "expert", None, "groups"),
        P(None, "expert", "groups"),
    )
    return jax.shard_map(
        per_device,
        mesh=mesh,
        in_specs=placed,
        out_specs=(P(("groups", "tensor", "expert"), None), P("expert", "groups")),
        check_vma=False,
    )
```

time: 30.4 us -> 30.4 us (level)
  no operation moved by 1% of the time
where the time goes in v3:
time: 30.4 us; the launch traced here: 30.2 us
  Pallas kernels  28 us (92%)
  local copies, waits for them, and re-layouts  1.55 us (5%)
  between operations  0.68 us (2%)
    pallas_call x1, Pallas kernels, per_device(): pl.pallas_call(functools.partial(kernel, experts, pair), out_shape=(jax.S...  26.1 us
    pallas_call x1, Pallas kernels, per_device(): pl.pallas_call(functools.partial(spread_kernel, experts, pair), out_shape...  1.86 us
    unnamed x8, local copies, waits for them, and re-layouts  1.55 us

profile of v3, /device:TPU:0, one launch (start us, length us, event | category | flops | bytes accessed | tf_op | source)
XLA Modules:
  0.0 30.2 jit_solution(7632398166809006873)
XLA Ops:
  0.6 0.0 copy-start.1
  0.6 0.0 copy-start.2
  0.7 26.1 %shard_map.104 = (bf16[512,256]{1,0:T(8,128)(2,1)}, f32[1,64]{1,0:T(1,128)}) custom-call(s32[1,2,4,8]{3,2,1,0:T(4,128)} %bitcast.4, s32[1,2,8]{2,1,0:T(2,128)} %bitcast.6, bf16[128,4096]{1,0:T(8,128)(2,1)} %d_hbm.1, bf16[1,704,2048]{2,1,0:T(8,128)(2,1)} %wd_hbm.1, bf16[1,704,2048]{2,1,0:T(8,128)(2,1)} %bitcast.8, bf16[1,704,2048]{2,1,0:T(8,128)(2,1)} %bitcast.9, ...), custom_call_target="tpu_custom_call" | custom-call | tf_op jit(solution)/shard_map/pallas_call | solution.py:294
  26.8 0.0 copy-done.1
  26.8 0.0 copy-done.2
  26.8 0.0 copy-start
  26.8 0.9 %copy-done = bf16[512,256]{1,0:T(8,128)(2,1)S(1)} copy-done((bf16[512,256]{1,0:T(8,128)(2,1)S(1)}, bf16[512,256]{1,0:T(8,128)(2,1)}, u32[]{:S(2)}) %copy-start) | copy-done | bytes 262168
  27.8 0.0 copy-start.3
  27.8 0.6 %copy-done.3 = f32[1,64]{1,0:T(1,128)S(1)} copy-done((f32[1,64]{1,0:T(1,128)S(1)}, f32[1,64]{1,0:T(1,128)}, u32[]{:S(2)}) %copy-start.3) | copy-done | bytes 280
  28.4 1.9 %shard_map.105 = (bf16[128,4096]{1,0:T(8,128)(2,1)}, f32[1,64]{1,0:T(1,128)}) custom-call(s32[1,2,4,8]{3,2,1,0:T(4,128)S(1)} %bitcast.5, s32[1,2,8]{2,1,0:T(2,128)S(1)} %bitcast.7, bf16[512,256]{1,0:T(8,128)(2,1)S(1)} %copy-done, f32[1,64]{1,0:T(1,128)S(1)} %copy-done.3), custom_call_target="tpu_custom_call" | custom-call | tf_op jit(solution)/shard_map/pallas_call | solution.py:337
Async XLA Ops:
  0.6 26.2 %copy-start.1 = (s32[8,1,2,4]{0,3,2,1:T(4,128)S(1)}, s32[8,1,2,4]{0,3,2,1:T(4,128)}, u32[]{:S(2)}) copy-start(s32[8,1,2,4]{0,3,2,1:T(4,128)} %param.16) | copy-start | bytes 772
  0.6 26.2 %copy-start.2 = (s32[8,1,2]{0,2,1:T(2,128)S(1)}, s32[8,1,2]{0,2,1:T(2,128)}, u32[]{:S(2)}) copy-start(s32[8,1,2]{0,2,1:T(2,128)} %param.17) | copy-start | bytes 196
  26.8 1.0 %copy-start = (bf16[512,256]{1,0:T(8,128)(2,1)S(1)}, bf16[512,256]{1,0:T(8,128)(2,1)}, u32[]{:S(2)}) copy-start(bf16[512,256]{1,0:T(8,128)(2,1)} %get-tuple-element.4.back) | copy-start | bytes 786436
  27.8 0.6 %copy-start.3 = (f32[1,64]{1,0:T(1,128)S(1)}, f32[1,64]{1,0:T(1,128)}, u32[]{:S(2)}) copy-start(f32[1,64]{1,0:T(1,128)} %get-tuple-element.5.scores) | copy-start | bytes 772

commit v4 on v3

--- a/solution.py
+++ b/solution.py
@@ -10,17 +10,13 @@
 MESH = pl.DeviceIdType.MESH
 TILE = 16
 LANES = 128
-SPLITS = 2
+SPLITS = 1
 F32 = jnp.float32
 BF16 = jnp.bfloat16
 
 
-def far_first(experts):
-    offsets = []
-    for step in range(experts):
-        offset = experts // 2 + ((step + 1) // 2 if step % 2 else -(step // 2))
-        offsets.append(offset % experts)
-    return [k for k in offsets if k] + [0]
+def offsets(experts):
+    return [k for k in range(1, experts)] + [0]
 
 
 def put(wide, start, count, values):
@@ -118,7 +114,7 @@
     piece = half // groups
     held = n * TILE
     tokens = d_v.shape[0]
-    order = far_first(experts)
+    order = offsets(experts)
 
     barrier = pltpu.get_barrier_semaphore()
     peers = []
@@ -347,7 +343,7 @@
             pltpu.VMEM(wide, F32),
             dma((2 * groups,)),
         ],
-        compiler_params=pltpu.CompilerParams(vmem_limit_bytes=40 * 1024 * 1024),
+        compiler_params=pltpu.CompilerParams(vmem_limit_bytes=63 * 1024 * 1024),
     )(routes, counts, back, scores)
 
 

time: 30.4 us -> 27 us (0.89)
  Pallas kernels: 28 us -> 26 us
  local copies, waits for them, and re-layouts: 1.55 us -> 0 us
    pallas_call x1, Pallas kernels: 26.1 us -> 23.2 us  [per_device(): pl.pallas_call(functools.partial(kernel, experts, pair), out_shape=(jax.S...]
    unnamed x8 -> x0, local copies, waits for them, and re-layouts: 1.55 us -> none
    pallas_call x1, Pallas kernels: 1.86 us -> 2.78 us  [per_device(): pl.pallas_call(functools.partial(spread_kernel, experts, pair), out_shape...]
where the time goes in v4:
time: 27 us; the launch traced here: 26.7 us
  Pallas kernels  26 us (96%)
  between operations  0.64 us (2%)
    pallas_call x1, Pallas kernels, per_device(): pl.pallas_call(functools.partial(kernel, experts, pair), out_shape=(jax.S...  23.2 us
    pallas_call x1, Pallas kernels, per_device(): pl.pallas_call(functools.partial(spread_kernel, experts, pair), out_shape...  2.78 us

profile of v4, /device:TPU:0, one launch (start us, length us, event | category | flops | bytes accessed | tf_op | source)
XLA Modules:
  0.0 26.7 jit_solution(13636502943075237309)
XLA Ops:
  0.6 23.2 %shard_map.104 = (bf16[256,512]{1,0:T(8,128)(2,1)}, f32[1,64]{1,0:T(1,128)}) custom-call(s32[1,2,4,8]{3,2,1,0:T(4,128)} %bitcast.6, s32[1,2,8]{2,1,0:T(2,128)} %bitcast.8, bf16[128,4096]{1,0:T(8,128)(2,1)} %d_hbm.1, bf16[1,704,2048]{2,1,0:T(8,128)(2,1)} %wd_hbm.1, bf16[1,704,2048]{2,1,0:T(8,128)(2,1)} %bitcast.4, bf16[1,704,2048]{2,1,0:T(8,128)(2,1)} %bitcast.5, ...), custom_call_target="tpu_custom_call" | custom-call | tf_op jit(solution)/shard_map/pallas_call | solution.py:290
  23.9 2.8 %shard_map.105 = (bf16[128,4096]{1,0:T(8,128)(2,1)}, f32[1,64]{1,0:T(1,128)}) custom-call(s32[1,2,4,8]{3,2,1,0:T(4,128)} %bitcast.7, s32[1,2,8]{2,1,0:T(2,128)} %bitcast.9, bf16[256,512]{1,0:T(8,128)(2,1)} %get-tuple-element.4.back, f32[1,64]{1,0:T(1,128)} %get-tuple-element.5.scores), custom_call_target="tpu_custom_call" | custom-call | tf_op jit(solution)/shard_map/pallas_call | solution.py:333
